TPU v7x, 32 devices: a whole 2x2x4 slice. The times are simulated.
32 devices in a mesh: groups: 2 (over x), tile: 16 (over z, y, core).
Axes of the slice: x: 2, y: 2, z: 4, core: 2. Of those that a mesh axis runs over, the one named last changes fastest.
Arguments:
- object_slices: float32 [3, 2, 4096, 512], P(None, None, ('groups', 'tile')), parts along dimension 2, may hold values from -1 to 1.3
- probe: float32 [4, 128, 128], P('groups'), parts along dimension 0, may hold values from -4.2 to 4.2
- propagator_phase: float32 [128, 128], replicated, may hold values from -3.140625 to 3.140625
- intensity: float32 [256, 128, 128], P(('groups', 'tile')), parts along dimension 0, may hold values from 0.1 to 3
- scan_rows: int32 [256], P(('groups', 'tile')), parts along dimension 0, may hold values from -32 to 32
- scan_cols: int32 [256], P(('groups', 'tile')), parts along dimension 0, may hold values from 0 to 384
Outputs:
- object_grad: float32 [3, 2, 4096, 512], P(None, None, ('groups', 'tile')), parts along dimension 2
- probe_grad: float32 [4, 128, 128], P('groups'), parts along dimension 0
There are 2 independent parts, one for each index of `groups`. A program takes and returns all parts, laid end to end along the dimension named above; an argument that names none is the same for every part. Nothing has to cross between parts.
All inputs are finite; a program needn't handle non-finite values.
Results may differ from a plain program's by a relative error of at most 0.0003.
Values sent between devices are 32-bit elements; how exact they have to be, the bound alone decides.
A program may use at most 64 MiB of HBM per device.

v0:
```python
import functools
import math

import jax
import jax.numpy as jnp
import ml_dtypes
import numpy as np
from jax import lax
from jax.experimental import pallas as pl
from jax.experimental.pallas import tpu as pltpu
from jax.sharding import PartitionSpec as P

HALO = 32
BF = jnp.bfloat16
F32 = jnp.float32


def dft_tables(n):
    k = np.arange(n)
    angle = -2.0 * math.pi * (k[:, None] * k[None, :] % n) / n
    re, im = np.cos(angle) / math.sqrt(n), np.sin(angle) / math.sqrt(n)
    a = np.block([[re, im], [-im, re]])

    def parts(m):
        hi = m.astype(ml_dtypes.bfloat16)
        lo = (m - hi.astype(np.float64)).astype(ml_dtypes.bfloat16)
        return hi, lo

    ahi, alo = parts(a)
    thi, tlo = parts(a.T)
    right = np.stack([np.concatenate([ahi, ahi, alo], 0), np.concatenate([thi, thi, tlo], 0)])
    left = np.stack([np.concatenate([thi, thi, tlo], 1), np.concatenate([ahi, ahi, alo], 1)])
    return right, left


def split(x):
    hi = x.astype(BF)
    lo = (x - hi.astype(F32)).astype(BF)
    return hi, lo


def rmul(x, right):
    hi, lo = split(x)
    return jnp.dot(jnp.concatenate([hi, lo, hi], axis=1), right, preferred_element_type=F32)


def lmul(x, left):
    hi, lo = split(x)
    return jnp.dot(left, jnp.concatenate([hi, lo, hi], axis=0), preferred_element_type=F32)


def flip(x, n):
    return jnp.concatenate(
        [
            jnp.concatenate([x[:n, :n], x[n:, :n]], axis=1),
            jnp.concatenate([x[:n, n:], x[n:, n:]], axis=1),
        ],
        axis=0,
    )


def cmul(ar, ai, br, bi):
    return ar * br - ai * bi, ar * bi + ai * br


def cmulc(ar, ai, br, bi):
    return ar * br + ai * bi, ai * br - ar * bi


def body(
    n, pairs, rows_ref, cols_ref, obj_ref, top_ref, bot_ref, probe_ref, ker_ref, img_ref, right_ref, left_ref,
    grad_ref, gtop_ref, gbot_ref, pg_ref, pad, acc, patch, psi,
):
    layers, _, own, width = obj_ref.shape
    blocks = width // n
    for b in range(blocks):
        cols = slice(b * n, (b + 1) * n)
        pad[:, :, b, :HALO] = top_ref[:, :, :, cols]
        pad[:, :, b, HALO : HALO + own] = obj_ref[:, :, :, cols]
        pad[:, :, b, HALO + own :] = bot_ref[:, :, :, cols]
    acc[...] = jnp.zeros_like(acc)
    pg_ref[...] = jnp.zeros_like(pg_ref)
    total = rows_ref.shape[0]

    def where(p):
        top = rows_ref[p] + HALO
        left = cols_ref[p]
        block = jnp.minimum(left // n, blocks - 2)
        return top, block, left - block * n

    def extract(p, s):
        top, block, off = where(p)
        shift = lax.rem(2 * n - off, 2 * n)
        for c in range(2):
            x = jnp.concatenate([pad[s, c, block + i, pl.ds(top, n), :] for i in range(2)], axis=1)
            patch[p, s, c] = pltpu.roll(x, shift, 1)[:, :n]

    def deposit(p, s, gr, gi):
        top, block, off = where(p)
        zero = jnp.zeros((n, n), F32)
        for c, g in enumerate((gr, gi)):
            v = pltpu.roll(jnp.concatenate([g, zero], axis=1), off, 1)
            acc[s, c, block, pl.ds(top, n), :] += v[:, :n]
            acc[s, c, block + 1, pl.ds(top, n), :] += v[:, n:]

    def join(waves):
        return jnp.concatenate([jnp.concatenate(w, axis=1) for w in waves], axis=0)

    def parts(x):
        return [(x[:n, :n], x[:n, n:]), (x[n:, :n], x[n:, n:])]

    def transform(x, way):
        y = rmul(x, right_ref[way])
        return flip(lmul(flip(y, n), left_ref[way]), n)

    def transform_all(xs, way):
        ys = [rmul(x, right_ref[way]) for x in xs]
        zs = [lmul(flip(y, n), left_ref[way]) for y in ys]
        return [flip(z, n) for z in zs]

    def step(g, carry):
        groups = [[(g * pairs + i) * 2 + j for j in range(2)] for i in range(pairs)]
        for s in range(layers):
            for group in groups:
                for p in group:
                    extract(p, s)
        waves = [[(probe_ref[0], probe_ref[1]) for p in group] for group in groups]
        for s in range(layers):
            waves = [
                [cmul(*w, patch[p, s, 0], patch[p, s, 1]) for p, w in zip(group, ws)]
                for group, ws in zip(groups, waves)
            ]
            spec = transform_all([join(ws) for ws in waves], 0)
            if s + 1 < layers:
                spec = [join([cmul(*w, ker_ref[0], ker_ref[1]) for w in parts(x)]) for x in spec]
                waves = [parts(x) for x in transform_all(spec, 1)]
                for group, ws in zip(groups, waves):
                    for p, w in zip(group, ws):
                        psi[p, s, 0] = w[0]
                        psi[p, s, 1] = w[1]
        back = []
        for group, x in zip(groups, spec):
            out = []
            for p, (fr, fi) in zip(group, parts(x)):
                e = 4.0 * (fr * fr + fi * fi - img_ref[p])
                out.append((e * fr, e * fi))
            back.append(join(out))
        for s in reversed(range(layers)):
            back = transform_all(back, 1)
            nxt = []
            for group, x in zip(groups, back):
                out = []
                for p, w in zip(group, parts(x)):
                    if s:
                        inc = psi[p, s - 1, 0], psi[p, s - 1, 1]
                    else:
                        inc = probe_ref[0], probe_ref[1]
                    deposit(p, s, *cmulc(*w, *inc))
                    out.append(cmulc(*w, patch[p, s, 0], patch[p, s, 1]))
                nxt.append(out)
            if s:
                spec = transform_all([join(ws) for ws in nxt], 0)
                back = [join([cmulc(*w, ker_ref[0], ker_ref[1]) for w in parts(x)]) for x in spec]
        for ws in nxt:
            for w in ws:
                pg_ref[0] += w[0]
                pg_ref[1] += w[1]
        return carry

    lax.fori_loop(0, total // (2 * pairs), step, 0)
    for b in range(blocks):
        cols = slice(b * n, (b + 1) * n)
        gtop_ref[:, :, :, cols] = acc[:, :, b, :HALO]
        grad_ref[:, :, :, cols] = acc[:, :, b, HALO : HALO + own]
        gbot_ref[:, :, :, cols] = acc[:, :, b, HALO + own :]


def core(scan_rows, scan_cols, obj, top, bot, probe, ker, intensity, pairs=4):
    layers, _, own, width = obj.shape
    n = probe.shape[1]
    total = scan_rows.shape[0]
    right, left = dft_tables(n)
    vmem = pl.BlockSpec(memory_space=pltpu.VMEM)
    smem = pl.BlockSpec(memory_space=pltpu.SMEM)
    return pl.pallas_call(
        functools.partial(body, n, pairs),
        out_shape=[
            jax.ShapeDtypeStruct(obj.shape, F32),
            jax.ShapeDtypeStruct((layers, 2, HALO, width), F32),
            jax.ShapeDtypeStruct((layers, 2, HALO, width), F32),
            jax.ShapeDtypeStruct(probe.shape, F32),
        ],
        in_specs=[smem, smem] + [vmem] * 8,
        out_specs=[vmem] * 4,
        scratch_shapes=[
            pltpu.VMEM((layers, 2, width // n, own + 2 * HALO, n), F32),
            pltpu.VMEM((layers, 2, width // n, own + 2 * HALO, n), F32),
            pltpu.VMEM((total, layers, 2, n, n), F32),
            pltpu.VMEM((total, layers - 1, 2, n, n), F32),
        ],
        compiler_params=pltpu.CompilerParams(vmem_limit_bytes=48 * 1024 * 1024),
    )(scan_rows, scan_cols, obj, top, bot, probe, ker, intensity, jnp.asarray(right), jnp.asarray(left))


def down(count):
    return [(i, (i + 1) % count) for i in range(count)]


def up(count):
    return [((i + 1) % count, i) for i in range(count)]


def local(object_slices, probe, propagator_phase, intensity, scan_rows, scan_cols):
    count = lax.axis_size("tile")
    own = object_slices.shape[2]
    ker = jnp.stack([jnp.cos(propagator_phase), jnp.sin(propagator_phase)])
    top = lax.ppermute(object_slices[:, :, own - HALO :], "tile", down(count))
    bot = lax.ppermute(object_slices[:, :, :HALO], "tile", up(count))
    grad, gtop, gbot, pg = core(scan_rows, scan_cols, object_slices, top, bot, probe, ker, intensity)
    from_below = lax.ppermute(gtop, "tile", up(count))
    from_above = lax.ppermute(gbot, "tile", down(count))
    grad = grad.at[:, :, :HALO].add(from_above)
    grad = grad.at[:, :, own - HALO :].add(from_below)
    total = lax.psum(pg, "tile")
    return grad, total / math.sqrt(count * scan_rows.shape[0])


def solution(mesh):
    placed = (
        P(None, None, ("groups", "tile"), None),
        P("groups", None, None),
        P(),
        P(("groups", "tile"), None, None),
        P(("groups", "tile")),
        P(("groups", "tile")),
    )
    return jax.shard_map(
        local,
        mesh=mesh,
        in_specs=placed,
        out_specs=(P(None, None, ("groups", "tile"), None), P("groups", None, None)),
        check_vma=False,
    )
```

profile of v0, /device:TPU:0, one launch (start us, length us, event | category | flops | bytes accessed | tf_op | source)
XLA Modules:
  0.0 141.6 jit_solution(16367548189169705101)
XLA Ops:
  7.2 0.0 copy-start
  7.2 0.0 copy-start.6
  7.2 0.0 copy-start.5
  7.2 0.0 copy-start.4
  7.2 0.0 all-reduce.2.cloned.1.call-start
  7.2 1.3 fusion.1
  8.5 5.5 %collective-permute-start.1 = (f32[3,2,32,512]{3,2,1,0:T(8,128)S(1)}, f32[3,2,32,512]{3,2,1,0:T(8,128)S(1)}, u32[]{:S(2)}, u32[]{:S(2)}) collective-permute-start(f32[3,2,32,512]{3,2,1,0:T(8,128)S(1)} %get-tuple-element.34), channel_id=1, source_target_pairs={{1,0},{2,1},{3,2},{4,3},{5,4},{6,5},{7,6},{8,7},{9,8},{10,9},{11,1... | collective-permute-start | bytes 1179656 | tf_op jit(solution)/shard_map/ppermute | solution.py:218
  14.0 0.0 collective-permute-start
  14.0 1.1 cosine_bitcast_fusion
  15.1 4.2 %collective-permute-done.1.bot_ref = f32[3,2,32,512]{3,2,1,0:T(8,128)S(1)} collective-permute-done((f32[3,2,32,512]{3,2,1,0:T(8,128)S(1)}, f32[3,2,32,512]{3,2,1,0:T(8,128)S(1)}, u32[]{:S(2)}, u32[]{:S(2)}) %collective-permute-start.1) | collective-permute-done | bytes 393248 | tf_op jit(solution)/shard_map/ppermute | solution.py:218
  19.3 4.6 %collective-permute-done.top_ref = f32[3,2,32,512]{3,2,1,0:T(8,128)S(1)} collective-permute-done((f32[3,2,32,512]{3,2,1,0:T(8,128)S(1)}, f32[3,2,32,512]{3,2,1,0:T(8,128)S(1)}, u32[]{:S(2)}, u32[]{:S(2)}) %collective-permute-start) | collective-permute-done | bytes 393248 | tf_op jit(solution)/shard_map/ppermute | solution.py:217
  23.9 0.0 copy-done
  23.9 0.0 copy-done.6
  23.9 0.0 copy-done.5
  23.9 0.0 copy-done.4
  24.0 0.0 copy-start.1
  24.0 1.1 copy-done.1
  25.1 0.0 copy-start.2
  25.1 1.1 copy-done.2
  26.2 0.0 copy-start.3
  26.2 1.0 copy-done.3
  27.3 14.1 %shard_map.95 = (f32[3,2,128,512]{3,2,1,0:T(8,128)}, f32[3,2,32,512]{3,2,1,0:T(8,128)S(1)}, f32[3,2,32,512]{3,2,1,0:T(8,128)S(1)}, f32[2,128,128]{2,1,0:T(8,128)}) custom-call(s32[8]{0:T(128)S(1)} %copy-done.5, s32[8]{0:T(128)S(1)} %copy-done.6, f32[3,2,128,512]{3,2,1,0:T(8,128)S(1)} %copy-done, f32[3,2,32,512]{3,2,1,0:T(8,128)S(1)} %collective-permute-done.top_ref, ...), custom_call_target="tpu_custom_call" | custom-call | tf_op jit(solution)/shard_map/pallas_call | solution.py:185
  41.4 0.0 collective-permute-start.2
  41.4 0.0 all-reduce.2.cloned.1.call-update
  41.4 4.5 %collective-permute-start.3 = (f32[3,2,32,512]{3,2,1,0:T(8,128)S(1)}, f32[3,2,32,512]{3,2,1,0:T(8,128)S(1)}, u32[]{:S(2)}, u32[]{:S(2)}) collective-permute-start(f32[3,2,32,512]{3,2,1,0:T(8,128)S(1)} %get-tuple-element.32), channel_id=1, source_target_pairs={{1,0},{2,1},{3,2},{4,3},{5,4},{6,5},{7,6},{8,7},{9,8},{10,9},{11,1... | collective-permute-start | bytes 1179656 | tf_op jit(solution)/shard_map/ppermute | solution.py:220
  45.9 83.7 %all-reduce.2.cloned.1.call-done = f32[2,128,128]{2,1,0:T(8,128)} async-done(((f32[2,128,128]{2,1,0:T(8,128)}), f32[2,128,128]{2,1,0:T(8,128)}) %all-reduce.2.cloned.1.call-update) | async-done | bytes 131088 | tf_op jit(solution)/shard_map/psum | solution.py:224
  129.6 1.6 %broadcast_multiply_fusion = f32[2,128,128]{2,1,0:T(8,128)} fusion(f32[2,128,128]{2,1,0:T(8,128)} %all-reduce.2.cloned.1.call-done), kind=kLoop, calls=%fused_computation.4 | loop fusion | flops 32768 | bytes 262144 | tf_op jit(solution)/shard_map/div | solution.py:225
  131.2 0.0 collective-permute-done.2
  131.2 1.8 %add_dynamic-update-slice_fusion = f32[3,2,128,512]{3,2,1,0:T(8,128)} fusion(f32[3,2,128,512]{3,2,1,0:T(8,128)} %get-tuple-element.30, f32[3,2,32,512]{3,2,1,0:T(8,128)S(1)} %collective-permute-done.2), kind=kLoop, calls=%fused_computation.2 | loop fusion | flops 98304 | bytes 1179648 | tf_op jit(solution)/shard_map/scatter-add | solution.py:222
  133.0 0.0 collective-permute-done.3
  133.0 1.8 %fusion = f32[3,2,128,512]{3,2,1,0:T(8,128)} fusion(f32[3,2,128,512]{3,2,1,0:T(8,128)} %add_dynamic-update-slice_fusion, f32[3,2,32,512]{3,2,1,0:T(8,128)S(1)} %collective-permute-done.3), kind=kLoop, calls=%fused_computation.1 | loop fusion | flops 98304 | bytes 1179648 | tf_op jit(solution)/shard_map/scatter-add | solution.py:223
  (1 shorter events, 0.0 us)
Async XLA Ops:
  7.2 16.8 %copy-start = (f32[3,2,128,512]{3,2,1,0:T(8,128)S(1)}, f32[3,2,128,512]{3,2,1,0:T(8,128)}, u32[]{:S(2)}) copy-start(f32[3,2,128,512]{3,2,1,0:T(8,128)} %obj_ref.1) | copy-start | bytes 4718596
  7.2 16.8 %copy-start.6 = (s32[8]{0:T(128)S(1)}, s32[8]{0:T(128)}, u32[]{:S(2)}) copy-start(s32[8]{0:T(128)} %cols_ref.1) | copy-start | bytes 100
  7.2 16.8 %copy-start.5 = (s32[8]{0:T(128)S(1)}, s32[8]{0:T(128)}, u32[]{:S(2)}) copy-start(s32[8]{0:T(128)} %rows_ref.1) | copy-start | bytes 100
  7.2 16.8 %copy-start.4 = (f32[2,128,128]{2,1,0:T(8,128)S(1)}, f32[2,128,128]{2,1,0:T(8,128)}, u32[]{:S(2)}) copy-start(f32[2,128,128]{2,1,0:T(8,128)} %probe_ref.1) | copy-start | bytes 393220
  7.2 122.4 %all-reduce.2.cloned.1.call-start = ((), (), s32[]{:S(2)}) async-start(), calls=%async_computation | async-start | bytes 262144 | tf_op jit(solution)/shard_map/psum | solution.py:224
  8.5 10.8 %collective-permute-start.1 = (f32[3,2,32,512]{3,2,1,0:T(8,128)S(1)}, f32[3,2,32,512]{3,2,1,0:T(8,128)S(1)}, u32[]{:S(2)}, u32[]{:S(2)}) collective-permute-start(f32[3,2,32,512]{3,2,1,0:T(8,128)S(1)} %get-tuple-element.34), channel_id=1, source_target_pairs={{1,0},{2,1},{3,2},{4,3},{5,4},{6,5},{7,6},{8,7},{9,8},{10,9},{11,1... | collective-permute-start | bytes 1179656 | tf_op jit(solution)/shard_map/ppermute | solution.py:218
  14.0 9.9 %collective-permute-start = (f32[3,2,32,512]{3,2,1,0:T(8,128)S(1)}, f32[3,2,32,512]{3,2,1,0:T(8,128)S(1)}, u32[]{:S(2)}, u32[]{:S(2)}) collective-permute-start(f32[3,2,32,512]{3,2,1,0:T(8,128)S(1)} %get-tuple-element.35), channel_id=1, source_target_pairs={{0,1},{1,2},{2,3},{3,4},{4,5},{5,6},{6,7},{7,8},{8,9},{9,10},{10,1... | collective-permute-start | bytes 1179656 | tf_op jit(solution)/shard_map/ppermute | solution.py:217
  24.0 1.1 copy-start.1
  25.1 1.1 copy-start.2
  26.2 1.0 copy-start.3
  41.4 89.8 %collective-permute-start.2 = (f32[3,2,32,512]{3,2,1,0:T(8,128)S(1)}, f32[3,2,32,512]{3,2,1,0:T(8,128)S(1)}, u32[]{:S(2)}, u32[]{:S(2)}) collective-permute-start(f32[3,2,32,512]{3,2,1,0:T(8,128)S(1)} %get-tuple-element.31), channel_id=1, source_target_pairs={{0,1},{1,2},{2,3},{3,4},{4,5},{5,6},{6,7},{7,8},{8,9},{9,10},{10,1... | collective-permute-start | bytes 1179656 | tf_op jit(solution)/shard_map/ppermute | solution.py:221
  41.4 91.6 %collective-permute-start.3 = (f32[3,2,32,512]{3,2,1,0:T(8,128)S(1)}, f32[3,2,32,512]{3,2,1,0:T(8,128)S(1)}, u32[]{:S(2)}, u32[]{:S(2)}) collective-permute-start(f32[3,2,32,512]{3,2,1,0:T(8,128)S(1)} %get-tuple-element.32), channel_id=1, source_target_pairs={{1,0},{2,1},{3,2},{4,3},{5,4},{6,5},{7,6},{8,7},{9,8},{10,9},{11,1... | collective-permute-start | bytes 1179656 | tf_op jit(solution)/shard_map/ppermute | solution.py:220
Sparse Core Ops, SparseCore 0:
  41.5 88.0 all-reduce.1
where the time goes:
time: 143 us; the launch traced here: 142 us
  waiting for transfers between devices  92.5 us (65%)
  Pallas kernels  14.1 us (10%)
  between operations  14.1 us (10%)
  starting transfers between devices  10 us (7%)
  local copies, waits for them, and re-layouts  5.68 us (4%)
  other arithmetic  5.18 us (4%)
    psum x1, waiting for transfers between devices, local(): total = lax.psum(pg, 'tile')  83.7 us
    pallas_call x1, Pallas kernels, core(): pl.pallas_call(functools.partial(body, n, pairs), out_shape=[jax.ShapeDty...  14.1 us
    ppermute x1, starting transfers between devices, local(): bot = lax.ppermute(object_slices[:, :, :HALO], 'tile', up(count))  5.5 us
    ppermute x1, waiting for transfers between devices, local(): top = lax.ppermute(object_slices[:, :, own - HALO:], 'tile', down(count))  4.6 us
    ppermute x1, starting transfers between devices, local(): from_below = lax.ppermute(gtop, 'tile', up(count))  4.49 us
    ppermute x1, waiting for transfers between devices, local(): bot = lax.ppermute(object_slices[:, :, :HALO], 'tile', up(count))  4.19 us
    unnamed x14, local copies, waits for them, and re-layouts  3.32 us
  transfers between devices with their start and end apart: 5, of which 3 were waited for; matrix products, arithmetic and copies ran while one was open for 3% of the time, Pallas kernels for 0%

commit v1 on v0

--- a/solution.py
+++ b/solution.py
@@ -202,27 +202,151 @@
     )(scan_rows, scan_cols, obj, top, bot, probe, ker, intensity, jnp.asarray(right), jnp.asarray(left))
 
 
-def down(count):
-    return [(i, (i + 1) % count) for i in range(count)]
-
-
-def up(count):
-    return [((i + 1) % count, i) for i in range(count)]
+def at(tile):
+    return dict(device_id={"tile": tile}, device_id_type=pl.DeviceIdType.MESH)
+
+
+def halo_body(count, obj_ref, phase_ref, top_ref, bot_ref, ker_ref, send, recv):
+    own = obj_ref.shape[2]
+    me = lax.axis_index("tile")
+    after, before = lax.rem(me + 1, count), lax.rem(me + count - 1, count)
+    barrier = pltpu.get_barrier_semaphore()
+    for peer in (before, after):
+        pl.semaphore_signal(barrier, inc=1, **at(peer))
+    pl.semaphore_wait(barrier, 2)
+    copies = [
+        pltpu.make_async_remote_copy(
+            src_ref=obj_ref.at[:, :, pl.ds(own - HALO, HALO)], dst_ref=top_ref,
+            send_sem=send.at[0], recv_sem=recv.at[0], **at(after),
+        ),
+        pltpu.make_async_remote_copy(
+            src_ref=obj_ref.at[:, :, pl.ds(0, HALO)], dst_ref=bot_ref,
+            send_sem=send.at[1], recv_sem=recv.at[1], **at(before),
+        ),
+    ]
+    for copy in copies:
+        copy.start()
+    ker_ref[0] = jnp.cos(phase_ref[...])
+    ker_ref[1] = jnp.sin(phase_ref[...])
+    for copy in copies:
+        copy.wait()
+
+
+def halo_exchange(obj, phase, count):
+    layers, _, _, width = obj.shape
+    edge = jax.ShapeDtypeStruct((layers, 2, HALO, width), F32)
+    anywhere = pl.BlockSpec(memory_space=pl.ANY)
+    vmem = pl.BlockSpec(memory_space=pltpu.VMEM)
+    return pl.pallas_call(
+        functools.partial(halo_body, count),
+        out_shape=[edge, edge, jax.ShapeDtypeStruct((2,) + phase.shape, F32)],
+        in_specs=[anywhere, vmem],
+        out_specs=[vmem] * 3,
+        scratch_shapes=[pltpu.SemaphoreType.DMA((2,)), pltpu.SemaphoreType.DMA((2,))],
+        compiler_params=pltpu.CompilerParams(
+            collective_id=0, has_side_effects=True, vmem_limit_bytes=8 * 1024 * 1024
+        ),
+    )(obj, phase)
+
+
+def reduce_body(
+    count, scale, grad_ref, gtop_ref, gbot_ref, pg_ref, out_ref, probe_ref,
+    edge, parts, piece, esend, erecv, ssend, srecv, gsend, grecv,
+):
+    own = grad_ref.shape[2]
+    me = lax.axis_index("tile")
+    after, before = lax.rem(me + 1, count), lax.rem(me + count - 1, count)
+    barrier = pltpu.get_barrier_semaphore()
+
+    def greet(d, c):
+        pl.semaphore_signal(barrier, inc=1, **at(lax.rem(me + d, count)))
+        return c
+
+    lax.fori_loop(1, count, greet, 0)
+    pl.semaphore_wait(barrier, count - 1)
+
+    def scatter(d):
+        peer = lax.rem(me + d, count)
+        return pltpu.make_async_remote_copy(
+            src_ref=pg_ref.at[peer], dst_ref=parts.at[d], send_sem=ssend.at[d], recv_sem=srecv.at[d], **at(peer)
+        )
+
+    def gather(d, slot):
+        peer = lax.rem(me + d, count)
+        return pltpu.make_async_remote_copy(
+            src_ref=piece, dst_ref=probe_ref.at[slot], send_sem=gsend.at[d], recv_sem=grecv.at[d], **at(peer)
+        )
+
+    def run(f):
+        def go(d, c):
+            f(d)
+            return c
+
+        lax.fori_loop(1, count, go, 0)
+
+    run(lambda d: scatter(d).start())
+    edges = [
+        pltpu.make_async_remote_copy(
+            src_ref=gbot_ref, dst_ref=edge.at[0], send_sem=esend.at[0], recv_sem=erecv.at[0], **at(after)
+        ),
+        pltpu.make_async_remote_copy(
+            src_ref=gtop_ref, dst_ref=edge.at[1], send_sem=esend.at[1], recv_sem=erecv.at[1], **at(before)
+        ),
+    ]
+    for copy in edges:
+        copy.start()
+    run(lambda d: scatter(d).wait_recv())
+
+    def add(d, total):
+        return total + parts[d]
+
+    piece[...] = lax.fori_loop(1, count, add, pg_ref[me]) * scale
+    run(lambda d: gather(d, me).start())
+    probe_ref[me] = piece[...]
+    out_ref[:, :, HALO : own - HALO] = grad_ref[:, :, HALO : own - HALO]
+    for copy in edges:
+        copy.wait_recv()
+    out_ref[:, :, :HALO] = grad_ref[:, :, :HALO] + edge[0]
+    out_ref[:, :, own - HALO :] = grad_ref[:, :, own - HALO :] + edge[1]
+    run(lambda d: gather(d, lax.rem(me + count - d, count)).wait_recv())
+    run(lambda d: scatter(d).wait_send())
+    run(lambda d: gather(d, me).wait_send())
+    for copy in edges:
+        copy.wait_send()
+
+
+def reduce_exchange(grad, gtop, gbot, pg, count, scale):
+    vmem = pl.BlockSpec(memory_space=pltpu.VMEM)
+    n = pg.shape[2]
+    rows = pg.shape[0] * pg.shape[1] // count
+    dma = pltpu.SemaphoreType.DMA
+    out, probe = pl.pallas_call(
+        functools.partial(reduce_body, count, scale),
+        out_shape=[
+            jax.ShapeDtypeStruct(grad.shape, F32),
+            jax.ShapeDtypeStruct((count, rows, n), F32),
+        ],
+        in_specs=[vmem] * 4,
+        out_specs=[vmem] * 2,
+        scratch_shapes=[
+            pltpu.VMEM((2,) + gtop.shape, F32),
+            pltpu.VMEM((count, rows, n), F32),
+            pltpu.VMEM((rows, n), F32),
+            dma((2,)), dma((2,)), dma((count,)), dma((count,)), dma((count,)), dma((count,)),
+        ],
+        compiler_params=pltpu.CompilerParams(
+            collective_id=1, has_side_effects=True, vmem_limit_bytes=24 * 1024 * 1024
+        ),
+    )(grad, gtop, gbot, pg.reshape(count, rows, n))
+    return out, probe.reshape(pg.shape)
 
 
 def local(object_slices, probe, propagator_phase, intensity, scan_rows, scan_cols):
     count = lax.axis_size("tile")
-    own = object_slices.shape[2]
-    ker = jnp.stack([jnp.cos(propagator_phase), jnp.sin(propagator_phase)])
-    top = lax.ppermute(object_slices[:, :, own - HALO :], "tile", down(count))
-    bot = lax.ppermute(object_slices[:, :, :HALO], "tile", up(count))
+    top, bot, ker = halo_exchange(object_slices, propagator_phase, count)
     grad, gtop, gbot, pg = core(scan_rows, scan_cols, object_slices, top, bot, probe, ker, intensity)
-    from_below = lax.ppermute(gtop, "tile", up(count))
-    from_above = lax.ppermute(gbot, "tile", down(count))
-    grad = grad.at[:, :, :HALO].add(from_above)
-    grad = grad.at[:, :, own - HALO :].add(from_below)
-    total = lax.psum(pg, "tile")
-    return grad, total / math.sqrt(count * scan_rows.shape[0])
+    scale = 1.0 / math.sqrt(count * scan_rows.shape[0])
+    return reduce_exchange(grad, gtop, gbot, pg, count, scale)
 
 
 def solution(mesh):

time: 143 us -> 51.8 us (0.36)
  waiting for transfers between devices: 92.5 us -> 0 us
  Pallas kernels: 14.1 us -> 44.8 us
  between operations: 14.1 us -> 0.71 us
  starting transfers between devices: 10 us -> 0 us
  other arithmetic: 5.18 us -> 0 us
    psum x1 -> x0, waiting for transfers between devices: 83.7 us -> none  [local(): total = lax.psum(pg, 'tile')]
    pallas_call x0 -> x2, Pallas kernels: none -> 31 us  [the longest x1 19.2 us: reduce_exchange(): pl.pallas_call(functools.partial(reduce_body, count, scale), out_shape=[j...]
    ppermute x4 -> x0, starting transfers between devices: 9.99 us -> none  [the longest x1 5.5 us: local(): bot = lax.ppermute(object_slices[:, :, :HALO], 'tile', up(count))]
    ppermute x4 -> x0, waiting for transfers between devices: 8.8 us -> none  [the longest x1 4.6 us: local(): top = lax.ppermute(object_slices[:, :, own - HALO:], 'tile', down(count))]
    scatter-add x2 -> x0, other arithmetic: 3.59 us -> none  [the longest x1 1.8 us: local(): grad = grad.at[:, :, :HALO].add(from_above)]
    unnamed x14 -> x18, local copies, waits for them, and re-layouts: 3.32 us -> 6 us
    div x1 -> x0, other arithmetic: 1.57 us -> none  [local(): return (grad, total / math.sqrt(count * scan_rows.shape[0]))]
  transfers between devices with their start and end apart: 5 -> 0, of which waited for: 3 -> 0; matrix products, arithmetic and copies ran while one was open for 3% -> 0% of each run, Pallas kernels for 0% -> 0%
where the time goes in v1:
time: 51.8 us; the launch traced here: 51.5 us
  Pallas kernels  44.8 us (86%)
  local copies, waits for them, and re-layouts  6 us (12%)
  between operations  0.71 us (1%)
    pallas_call x1, Pallas kernels, reduce_exchange(): pl.pallas_call(functools.partial(reduce_body, count, scale), out_shape=[j...  19.2 us
    pallas_call x1, Pallas kernels, core(): pl.pallas_call(functools.partial(body, n, pairs), out_shape=[jax.ShapeDty...  13.8 us
    pallas_call x1, Pallas kernels, halo_exchange(): pl.pallas_call(functools.partial(halo_body, count), out_shape=[edge, edge...  11.8 us
    unnamed x18, local copies, waits for them, and re-layouts  6 us

profile of v1, /device:TPU:0, one launch (start us, length us, event | category | flops | bytes accessed | tf_op | source)
XLA Modules:
  0.0 51.5 jit_solution(16919177980981842051)
XLA Ops:
  0.6 0.0 copy-start
  0.6 1.4 %copy-done = f32[3,2,128,512]{3,2,1,0:T(8,128)S(1)} copy-done((f32[3,2,128,512]{3,2,1,0:T(8,128)S(1)}, f32[3,2,128,512]{3,2,1,0:T(8,128)}, u32[]{:S(2)}) %copy-start) | copy-done | bytes 1572888
  2.0 0.0 copy-start.5
  2.0 0.8 %copy-done.5 = f32[128,128]{1,0:T(8,128)S(1)} copy-done((f32[128,128]{1,0:T(8,128)S(1)}, f32[128,128]{1,0:T(8,128)}, u32[]{:S(2)}) %copy-start.5) | copy-done | bytes 65560
  2.9 0.0 copy-start.1
  2.9 0.0 copy-start.2
  2.9 0.0 copy-start.6
  2.9 0.0 copy-start.7
  2.9 11.8 %shard_map.95 = (f32[3,2,32,512]{3,2,1,0:T(8,128)S(1)}, f32[3,2,32,512]{3,2,1,0:T(8,128)S(1)}, f32[2,128,128]{2,1,0:T(8,128)S(1)}) custom-call(f32[3,2,128,512]{3,2,1,0:T(8,128)S(1)} %copy-done, f32[128,128]{1,0:T(8,128)S(1)} %copy-done.5), custom_call_target="tpu_custom_call" | custom-call | tf_op jit(solution)/shard_map/pallas_call | solution.py:240
  14.7 0.0 copy-done.1
  14.7 0.0 copy-done.2
  14.7 0.0 copy-done.6
  14.7 0.0 copy-done.7
  14.7 0.0 copy-start.3
  14.7 1.0 %copy-done.3 = f32[8,128,128]{2,1,0:T(8,128)S(1)} copy-done((f32[8,128,128]{2,1,0:T(8,128)S(1)}, f32[8,128,128]{2,1,0:T(8,128)}, u32[]{:S(2)}) %copy-start.3) | copy-done | bytes 524312
  15.8 0.0 copy-start.4
  15.8 0.9 %copy-done.4 = f32[2,128,128]{2,1,0:T(8,128)S(1)} copy-done((f32[2,128,128]{2,1,0:T(8,128)S(1)}, f32[2,128,128]{2,1,0:T(8,128)}, u32[]{:S(2)}) %copy-start.4) | copy-done | bytes 131096
  16.7 13.8 %shard_map.96 = (f32[3,2,128,512]{3,2,1,0:T(8,128)S(1)}, f32[3,2,32,512]{3,2,1,0:T(8,128)S(1)}, f32[3,2,32,512]{3,2,1,0:T(8,128)S(1)}, f32[2,128,128]{2,1,0:T(8,128)S(1)}) custom-call(s32[8]{0:T(128)S(1)} %copy-done.6, s32[8]{0:T(128)S(1)} %copy-done.7, f32[3,2,128,512]{3,2,1,0:T(8,128)} %obj_ref.3, f32[3,2,32,512]{3,2,1,0:T(8,128)S(1)} %get-tuple-element.11.top_ref, ...), custom_call_target="tpu_custom_call" | custom-call | tf_op jit(solution)/shard_map/pallas_call | solution.py:185
  30.5 19.2 %shard_map.97 = (f32[3,2,128,512]{3,2,1,0:T(8,128)S(1)}, f32[16,16,128]{2,1,0:T(8,128)S(1)}) custom-call(f32[3,2,128,512]{3,2,1,0:T(8,128)S(1)} %get-tuple-element.14.grad_ref, f32[3,2,32,512]{3,2,1,0:T(8,128)S(1)} %get-tuple-element.15.gtop_ref, f32[3,2,32,512]{3,2,1,0:T(8,128)S(1)} %get-tuple-element.16.gbot_ref, f32[16,16,128]{2,1,0:T(8,128)S(1)} %bitcast.2), custom_call_target="tpu_custom_call" | custom-call | tf_op jit(solution)/shard_map/pallas_call | solution.py:323
  49.7 1.1 %copy.12 = f32[3,2,128,512]{3,2,1,0:T(8,128)} copy(f32[3,2,128,512]{3,2,1,0:T(8,128)S(1)} %get-tuple-element.22) | data formatting | bytes 3145728
  50.8 0.7 %copy.13 = f32[2,128,128]{2,1,0:T(8,128)} copy(f32[2,128,128]{2,1,0:T(8,128)S(1)} %bitcast.3) | data formatting | bytes 262144
Async XLA Ops:
  0.6 1.4 %copy-start = (f32[3,2,128,512]{3,2,1,0:T(8,128)S(1)}, f32[3,2,128,512]{3,2,1,0:T(8,128)}, u32[]{:S(2)}) copy-start(f32[3,2,128,512]{3,2,1,0:T(8,128)} %obj_ref.3) | copy-start | bytes 4718596
  2.0 0.8 %copy-start.5 = (f32[128,128]{1,0:T(8,128)S(1)}, f32[128,128]{1,0:T(8,128)}, u32[]{:S(2)}) copy-start(f32[128,128]{1,0:T(8,128)} %phase_ref.1) | copy-start | bytes 196612
  2.9 11.8 %copy-start.1 = (bf16[2,256,768]{2,1,0:T(8,128)(2,1)S(1)}, bf16[2,256,768]{2,1,0:T(8,128)(2,1)}, u32[]{:S(2)}) copy-start(bf16[2,256,768]{2,1,0:T(8,128)(2,1)} %constant.5.clone.left_ref) | copy-start | bytes 2359300
  2.9 11.8 %copy-start.2 = (bf16[2,768,256]{2,1,0:T(8,128)(2,1)S(1)}, bf16[2,768,256]{2,1,0:T(8,128)(2,1)}, u32[]{:S(2)}) copy-start(bf16[2,768,256]{2,1,0:T(8,128)(2,1)} %constant.4.clone.right_ref) | copy-start | bytes 2359300
  2.9 11.8 %copy-start.6 = (s32[8]{0:T(128)S(1)}, s32[8]{0:T(128)}, u32[]{:S(2)}) copy-start(s32[8]{0:T(128)} %rows_ref.1) | copy-start | bytes 100
  2.9 11.8 %copy-start.7 = (s32[8]{0:T(128)S(1)}, s32[8]{0:T(128)}, u32[]{:S(2)}) copy-start(s32[8]{0:T(128)} %cols_ref.1) | copy-start | bytes 100
  14.7 1.0 %copy-start.3 = (f32[8,128,128]{2,1,0:T(8,128)S(1)}, f32[8,128,128]{2,1,0:T(8,128)}, u32[]{:S(2)}) copy-start(f32[8,128,128]{2,1,0:T(8,128)} %img_ref.1) | copy-start | bytes 1572868
  15.8 0.9 %copy-start.4 = (f32[2,128,128]{2,1,0:T(8,128)S(1)}, f32[2,128,128]{2,1,0:T(8,128)}, u32[]{:S(2)}) copy-start(f32[2,128,128]{2,1,0:T(8,128)} %probe_ref.1) | copy-start | bytes 393220
